TPU v7x, 256 devices: a whole 4x4x8 slice. The times are simulated.
256 devices in a mesh: pipe: 8 (over x, y_hi), ctx: 32 (over y_lo, z, core).
Axes of the slice: x: 4, y: 4 (y_hi: 2, y_lo: 2; y = y_hi * 2 + y_lo), z: 8, core: 2. Of those that a mesh axis runs over, the one named last changes fastest.
Arguments:
- stored_acts: bfloat16 [8, 4096, 1024], P('pipe', 'ctx'), may hold values from -6 to 6
- queries: bfloat16 [8, 4096, 1024], P('pipe', 'ctx'), may hold values from -40 to 40
- patch_times: int32 [8, 4096], P('pipe', 'ctx'), may hold values from 0 to 31, as said below
- key_gain: float32 [8, 1024], P('pipe'), may hold values from 0.5 to 2
- value_gain: float32 [8, 1024], P('pipe'), may hold values from 0.5 to 2
- conv_weight: bfloat16 [8, 27, 128, 128], P('pipe'), may hold values from -0.109375 to 0.109375
- prior_grad: bfloat16 [8, 4096, 1024], P('pipe', 'ctx'), may hold values from -6 to 6
- loss_grad: bfloat16 [4096, 1024], P('ctx'), may hold values from -6 to 6
Outputs:
- input_grad: bfloat16 [8, 4096, 1024], P('pipe', 'ctx')
Inputs may be any that keep to these rules, and one draw needn't show every extreme that they name: `patch_times`: within each aligned group of four patches of a sequence, no patch has a later time step than the first of the group.
All inputs are finite; a program needn't handle non-finite values.
Results may differ from a plain program's by a relative error of at most 0.012.
Values may be sent and summed in bfloat16 or wider, within the bound.
No kernel may reach another device: no remote copies, remote signals or barrier semaphores. Data moves between devices by JAX's collectives and lax.ppermute only.
A program may use at most 128 MiB of HBM per device.

v0:
```python
import math
import jax
import jax.numpy as jnp
from jax import lax
from jax.sharding import PartitionSpec as P

HEADS = 16
HEAD_DIM = 64
CHANNELS = 128
GY = 8
GZ = 8
D = 1024
FIELDS = 8


def shifted(value, axis, steps):
    count = lax.axis_size(axis)
    leading, last = (max(0, -steps), min(count, count - steps))
    return lax.ppermute(value, axis, [(source, source + steps) for source in range(leading, last)])


def padded_2(block, sides, width):
    for axis, dim in sides:
        count = lax.axis_size(axis)
        forward = [(i, i + 1) for i in range(count - 1)]
        backward = [(target, source) for source, target in forward]
        low = lax.ppermute(
            lax.slice_in_dim(block, block.shape[dim] - width, None, axis=dim), axis, forward
        )
        high = lax.ppermute(lax.slice_in_dim(block, 0, width, axis=dim), axis, backward)
        block = jnp.concatenate([low, block, high], axis=dim)
    return block


def conv_backward(extended, weight, row_count):
    planes = row_count // (GY * GZ)
    grid_field = extended.reshape(planes + 2, GY, GZ, FIELDS, CHANNELS)
    padded = jnp.pad(grid_field, ((0, 0), (1, 1), (1, 1), (0, 0), (0, 0)))
    windows = []
    for shift_x in (-1, 0, 1):
        for shift_y in (-1, 0, 1):
            for shift_z in (-1, 0, 1):
                windows.append(
                    padded[
                        1 - shift_x : 1 - shift_x + planes,
                        1 - shift_y : 1 - shift_y + GY,
                        1 - shift_z : 1 - shift_z + GZ,
                    ]
                )
    stacked = jnp.stack(windows, axis=4).reshape(row_count * FIELDS, 27 * CHANNELS)
    matrix = jnp.transpose(weight, (0, 2, 1)).reshape(27 * CHANNELS, CHANNELS)
    return jnp.dot(stacked, matrix, preferred_element_type=jnp.float32).reshape(row_count, D)


def split_heads(matrix):
    return matrix.reshape(matrix.shape[0], HEADS, matrix.shape[1] // HEADS)


def keys_values(rows_x, key_scale, value_scale):
    widened = rows_x.astype(jnp.float32)
    keyed = split_heads((widened * key_scale).astype(jnp.bfloat16))
    valued = jnp.roll(split_heads((widened * value_scale).astype(jnp.bfloat16)), HEADS // 2, axis=1)
    return (keyed, valued)


def masked_scores(query_heads, key_heads, query_times, key_times):
    scores = jnp.einsum(
        "qhe,khe->qhk", query_heads, key_heads, preferred_element_type=jnp.float32
    ) * HEAD_DIM ** (-0.5)
    visible = key_times[None, None, :] <= query_times[:, None, None]
    return jnp.where(visible, scores, -jnp.inf)


def running_stats(running, query_heads, grad_heads, query_times, key_heads, value_heads, key_times):
    running_max, running_sum, weighted = running
    scores = masked_scores(query_heads, key_heads, query_times, key_times)
    prob_grad = jnp.einsum(
        "qhe,khe->qhk", grad_heads, value_heads, preferred_element_type=jnp.float32
    )
    new_max = jnp.maximum(running_max, jnp.max(scores, axis=2))
    exponent = jnp.exp(scores - new_max[:, :, None])
    factor = jnp.exp(running_max - new_max)
    return (
        new_max,
        running_sum * factor + jnp.sum(exponent, axis=2),
        weighted * factor + jnp.sum(exponent * prob_grad, axis=2),
    )


def key_terms(
    query_heads,
    grad_heads,
    query_times,
    log_total,
    delta_rows,
    key_heads,
    value_heads,
    key_times,
    key_scale,
    value_scale,
):
    scores = masked_scores(query_heads, key_heads, query_times, key_times)
    probability = jnp.exp(scores - log_total[:, :, None])
    prob_grad = jnp.einsum(
        "qhe,khe->qhk", grad_heads, value_heads, preferred_element_type=jnp.float32
    )
    score_grad = (probability * (prob_grad - delta_rows[:, :, None])).astype(jnp.bfloat16)
    value_grad = jnp.einsum(
        "qhk,qhe->khe",
        probability.astype(jnp.bfloat16),
        grad_heads,
        preferred_element_type=jnp.float32,
    )
    key_grad = jnp.einsum(
        "qhk,qhe->khe", score_grad, query_heads, preferred_element_type=jnp.float32
    ) * HEAD_DIM ** (-0.5)
    key_count = key_heads.shape[0]
    return (
        key_grad.reshape(key_count, -1) * key_scale
        + jnp.roll(value_grad, HEADS // 2, axis=1).reshape(key_count, -1) * value_scale
    )


def on_device(
    stored_acts, queries, patch_times, key_gain, value_gain, conv_weight, prior_grad, loss_grad
):
    own_acts = stored_acts[0]
    own_queries = queries[0]
    own_times = patch_times[0].astype(jnp.float32)
    time_wire = patch_times[0].astype(jnp.bfloat16)
    key_scale = key_gain[0]
    value_scale = value_gain[0]
    row_count = own_acts.shape[0]
    feature_count = own_acts.shape[1]
    arrived = shifted(prior_grad[0], "pipe", -1)
    is_last = lax.axis_index("pipe") == lax.axis_size("pipe") - 1
    incoming = jnp.where(is_last, loss_grad, arrived)
    extended = padded_2(incoming, (("ctx", 0),), GY * GZ)
    conv_part = conv_backward(extended, conv_weight[0], row_count)
    query_heads = split_heads(own_queries)
    grad_heads = split_heads(incoming)
    start_stats = (
        jnp.full((row_count, HEADS), -1e30, jnp.float32),
        jnp.zeros((row_count, HEADS), jnp.float32),
        jnp.zeros((row_count, HEADS), jnp.float32),
    )

    def sweep_keys(running, segment):
        key_heads, value_heads = keys_values(segment[0], key_scale, value_scale)
        return (
            running_stats(
                running,
                query_heads,
                grad_heads,
                own_times,
                key_heads,
                value_heads,
                segment[1].astype(jnp.float32),
            ),
            None,
        )

    shard_part = (
        lax.all_gather(own_acts, "ctx", axis=0, tiled=True),
        lax.all_gather(time_wire, "ctx", axis=0, tiled=True),
    )
    running = start_stats
    segment_x = shard_part[0]
    length = segment_x.shape[0]
    block_size = math.gcd(length, 512)
    running, _ = lax.scan(
        sweep_keys,
        running,
        (
            segment_x.reshape(length // block_size, block_size, feature_count),
            shard_part[1].reshape(length // block_size, block_size),
        ),
    )
    running_max, running_sum, weighted = running
    log_total = running_max + jnp.log(running_sum)
    delta_rows = weighted / running_sum
    all_total, all_delta, all_times = (
        lax.all_gather(log_total, "ctx", axis=0, tiled=True),
        lax.all_gather(delta_rows, "ctx", axis=0, tiled=True),
        lax.all_gather(own_times, "ctx", axis=0, tiled=True),
    )
    own_keys, own_values = keys_values(own_acts, key_scale, value_scale)

    def sweep_queries(accumulated, segment):
        segment_q, segment_g, segment_times, segment_total, segment_delta = segment
        return (
            accumulated
            + key_terms(
                split_heads(segment_q),
                split_heads(segment_g),
                segment_times,
                segment_total,
                segment_delta,
                own_keys,
                own_values,
                own_times,
                key_scale,
                value_scale,
            ),
            None,
        )

    accumulated = jnp.zeros((row_count, feature_count), jnp.float32)
    shard_part = (
        lax.all_gather(own_queries, "ctx", axis=0, tiled=True),
        lax.all_gather(incoming, "ctx", axis=0, tiled=True),
    )
    length = shard_part[0].shape[0]
    block_size = math.gcd(length, 512)
    block_count = length // block_size
    segments = (
        shard_part[0].reshape(block_count, block_size, feature_count),
        shard_part[1].reshape(block_count, block_size, feature_count),
        all_times.reshape(block_count, block_size),
        all_total.reshape(block_count, block_size, HEADS),
        all_delta.reshape(block_count, block_size, HEADS),
    )
    accumulated, _ = lax.scan(sweep_queries, accumulated, segments)
    return (conv_part + accumulated).astype(jnp.bfloat16)[None]


def solution(mesh):
    in_specs = (
        P("pipe", "ctx", None),
        P("pipe", "ctx", None),
        P("pipe", "ctx"),
        P("pipe", None),
        P("pipe", None),
        P("pipe", None, None, None),
        P("pipe", "ctx", None),
        P("ctx", None),
    )
    out_specs = P("pipe", "ctx", None)
    return jax.shard_map(
        on_device, mesh=mesh, in_specs=in_specs, out_specs=out_specs, check_vma=False
    )
```

profile of v0, /device:TPU:29, one launch (start us, length us, event | category | flops | bytes accessed | tf_op | source)
XLA Modules:
  0.0 412.9 jit_solution(16347624726571813158)
XLA Ops:
  8.4 2.9 collective-permute-start
  12.4 7.5 %collective-permute-done = bf16[128,1024]{0,1:T(8,128)(2,1)S(1)} collective-permute-done((bf16[128,1024]{0,1:T(8,128)(2,1)S(1)}, bf16[128,1024]{0,1:T(8,128)(2,1)S(1)}, u32[]{:S(2)}, u32[]{:S(2)}) %collective-permute-start) | collective-permute-done | bytes 262176 | tf_op jit(solution)/shard_map/ppermute | solution.py:19
  22.5 1.8 copy.78
  29.7 5.0 %collective-permute-start.1 = (bf16[64,1024]{0,1:T(8,128)(2,1)S(1)}, bf16[64,1024]{0,1:T(8,128)(2,1)S(1)}, u32[]{:S(2)}, u32[]{:S(2)}) collective-permute-start(bf16[64,1024]{0,1:T(8,128)(2,1)S(1)} %get-tuple-element.327), channel_id=1, source_target_pairs={{0,1},{1,2},{2,3},{3,4},{4,5},{5,6},{6,7},{7,8},{8,9},{9,10},{10,1... | collective-permute-start | bytes 393224 | tf_op jit(solution)/shard_map/ppermute | solution.py:27
  34.7 1.9 collective-permute-start.2
  36.6 39.2 %all-gather.2 = bf16[1,4096]{1,0:T(2,128)(2,1)S(1)} all-gather(bf16[1,128]{1,0:T(2,128)(2,1)S(1)} %get-tuple-element.331), channel_id=4, replica_groups=mesh['pipe'=8,'ctx'=32] {'ctx'}, dimensions={1}, use_global_device_ids=true | all-gather | bytes 8448 | tf_op jit(solution)/shard_map/all_gather | solution.py:165
  75.9 30.5 %all-gather.1 = f32[1,4096]{1,0:T(1,128)S(1)} all-gather(f32[1,128]{1,0:T(1,128)S(1)} %get-tuple-element.333), channel_id=3, replica_groups=mesh['pipe'=8,'ctx'=32] {'ctx'}, dimensions={1}, use_global_device_ids=true | all-gather | bytes 16896 | tf_op jit(solution)/shard_map/all_gather | solution.py:185
  107.6 2.3 copy.76
  115.3 2.0 fusion.93
  118.2 65.1 %while.26 = (s32[]{:T(128)}, f32[128,16]{0,1:T(8,128)S(1)}, f32[128,16]{0,1:T(8,128)S(1)}, f32[128,16]{0,1:T(8,128)S(1)}, bf16[8,512]{1,0:T(8,128)(2,1)S(1)}, /*...) while((s32[]{:T(128)}, f32[128,16]{0,1:T(8,128)S(1)}, ...), condition=%wide.region_4.5_spmd.clone, body=%wide.region_0.4_spmd.clone.sunk | while | flops 284768768 | bytes 24049328 | solution.py:171
  123.9 1.6 fusion.131
  183.4 33.4 %all_gather.27 = f32[4096,16]{0,1:T(8,128)S(1)} all-gather(f32[128,16]{0,1:T(8,128)S(1)} %get-tuple-element.329), channel_id=1, replica_groups=mesh['pipe'=8,'ctx'=32] {'ctx'}, dimensions={0}, use_global_device_ids=true | all-gather | bytes 270336 | tf_op jit(solution)/shard_map/all_gather | solution.py:184
  217.6 32.4 %all_gather.25 = f32[4096,16]{0,1:T(8,128)S(1)} all-gather(f32[128,16]{0,1:T(8,128)S(1)} %get-tuple-element.330), channel_id=1, replica_groups=mesh['pipe'=8,'ctx'=32] {'ctx'}, dimensions={0}, use_global_device_ids=true | all-gather | bytes 270336 | tf_op jit(solution)/shard_map/all_gather | solution.py:183
  250.9 12.0 %copy.80 = bf16[4096,1024]{1,0:T(8,128)(2,1)} copy(bf16[4096,1024]{0,1:T(8,128)(2,1)} %all-gather.8.cloned.1.call-done) | data formatting | bytes 16777216 | tf_op jit(solution)/shard_map/all_gather | solution.py:211
  262.9 140.5 %while.27 = (s32[]{:T(128)}, f32[128,1024]{0,1:T(8,128)}, bf16[8,512,1024]{2,1,0:T(8,128)(2,1)}, f32[128]{0:T(128)S(1)}, f32[8,512]{1,0:T(8,128)}, /*index=5*/bf...) while((s32[]{:T(128)}, f32[128,1024]{0,1:T(8,128)}, ...), condition=%wide.region_6.7_spmd.clone, body=%wide.region_5.6_spmd.clone.sunk | while | flops 548339712 | bytes 35699416 | solution.py:223
  264.9 1.7 constant_dynamic-slice_fusion.11
  267.7 2.8 fusion.141
  270.4 5.4 %fusion.142 = f32[16,64,128]{2,1,0:T(8,128)S(1)} fusion(bf16[512,16,64]{0,2,1:T(8,128)(2,1)S(1)} %bitcast.339, f32[16,512,128]{2,1,0:T(8,128)} %fusion.141, bf16[512,16,64]{0,2,1:T(8,128)(2,1)S(1)} %bitcast.340, bf16[128,16,64]{0,2,1:T(8,128)(2,1)} %get-tuple-element.576, f32[512,16]{0,1:T(8,128)S(1)} %bitcast.359, f32[512,16]{0,1:T(8,128)S(1)} %bitcast.357, ...), kind=kOutput, calls=%fused_computation.13.clone.1 | convolution fusion | flops 274857984 | bytes 7208960 | tf_op jit(solution)/shard_map/while/body/eval_jaxpr/qhk,qhe->khe/dot_general | solution.py:114
  275.8 3.2 fusion.143
  282.4 1.8 constant_dynamic-slice_fusion.11
  285.3 2.8 fusion.141
  288.0 5.4 %fusion.142 = f32[16,64,128]{2,1,0:T(8,128)S(1)} fusion(bf16[512,16,64]{0,2,1:T(8,128)(2,1)S(1)} %bitcast.339, f32[16,512,128]{2,1,0:T(8,128)} %fusion.141, bf16[512,16,64]{0,2,1:T(8,128)(2,1)S(1)} %bitcast.340, bf16[128,16,64]{0,2,1:T(8,128)(2,1)} %get-tuple-element.576, f32[512,16]{0,1:T(8,128)S(1)} %bitcast.359, f32[512,16]{0,1:T(8,128)S(1)} %bitcast.357, ...), kind=kOutput, calls=%fused_computation.13.clone.1 | convolution fusion | flops 274857984 | bytes 7208960 | tf_op jit(solution)/shard_map/while/body/eval_jaxpr/qhk,qhe->khe/dot_general | solution.py:114
  293.4 3.2 fusion.143
  300.0 1.7 constant_dynamic-slice_fusion.11
  302.8 2.8 fusion.141
  305.6 5.4 %fusion.142 = f32[16,64,128]{2,1,0:T(8,128)S(1)} fusion(bf16[512,16,64]{0,2,1:T(8,128)(2,1)S(1)} %bitcast.339, f32[16,512,128]{2,1,0:T(8,128)} %fusion.141, bf16[512,16,64]{0,2,1:T(8,128)(2,1)S(1)} %bitcast.340, bf16[128,16,64]{0,2,1:T(8,128)(2,1)} %get-tuple-element.576, f32[512,16]{0,1:T(8,128)S(1)} %bitcast.359, f32[512,16]{0,1:T(8,128)S(1)} %bitcast.357, ...), kind=kOutput, calls=%fused_computation.13.clone.1 | convolution fusion | flops 274857984 | bytes 7208960 | tf_op jit(solution)/shard_map/while/body/eval_jaxpr/qhk,qhe->khe/dot_general | solution.py:114
  310.9 3.2 fusion.143
  317.6 1.7 constant_dynamic-slice_fusion.11
  320.4 2.8 fusion.141
  323.1 5.4 %fusion.142 = f32[16,64,128]{2,1,0:T(8,128)S(1)} fusion(bf16[512,16,64]{0,2,1:T(8,128)(2,1)S(1)} %bitcast.339, f32[16,512,128]{2,1,0:T(8,128)} %fusion.141, bf16[512,16,64]{0,2,1:T(8,128)(2,1)S(1)} %bitcast.340, bf16[128,16,64]{0,2,1:T(8,128)(2,1)} %get-tuple-element.576, f32[512,16]{0,1:T(8,128)S(1)} %bitcast.359, f32[512,16]{0,1:T(8,128)S(1)} %bitcast.357, ...), kind=kOutput, calls=%fused_computation.13.clone.1 | convolution fusion | flops 274857984 | bytes 7208960 | tf_op jit(solution)/shard_map/while/body/eval_jaxpr/qhk,qhe->khe/dot_general | solution.py:114
  328.5 3.2 fusion.143
  335.1 1.7 constant_dynamic-slice_fusion.11
  337.9 2.8 fusion.141
  340.7 5.4 %fusion.142 = f32[16,64,128]{2,1,0:T(8,128)S(1)} fusion(bf16[512,16,64]{0,2,1:T(8,128)(2,1)S(1)} %bitcast.339, f32[16,512,128]{2,1,0:T(8,128)} %fusion.141, bf16[512,16,64]{0,2,1:T(8,128)(2,1)S(1)} %bitcast.340, bf16[128,16,64]{0,2,1:T(8,128)(2,1)} %get-tuple-element.576, f32[512,16]{0,1:T(8,128)S(1)} %bitcast.359, f32[512,16]{0,1:T(8,128)S(1)} %bitcast.357, ...), kind=kOutput, calls=%fused_computation.13.clone.1 | convolution fusion | flops 274857984 | bytes 7208960 | tf_op jit(solution)/shard_map/while/body/eval_jaxpr/qhk,qhe->khe/dot_general | solution.py:114
  346.1 3.2 fusion.143
  352.7 1.7 constant_dynamic-slice_fusion.11
  355.5 2.8 fusion.141
  358.3 5.4 %fusion.142 = f32[16,64,128]{2,1,0:T(8,128)S(1)} fusion(bf16[512,16,64]{0,2,1:T(8,128)(2,1)S(1)} %bitcast.339, f32[16,512,128]{2,1,0:T(8,128)} %fusion.141, bf16[512,16,64]{0,2,1:T(8,128)(2,1)S(1)} %bitcast.340, bf16[128,16,64]{0,2,1:T(8,128)(2,1)} %get-tuple-element.576, f32[512,16]{0,1:T(8,128)S(1)} %bitcast.359, f32[512,16]{0,1:T(8,128)S(1)} %bitcast.357, ...), kind=kOutput, calls=%fused_computation.13.clone.1 | convolution fusion | flops 274857984 | bytes 7208960 | tf_op jit(solution)/shard_map/while/body/eval_jaxpr/qhk,qhe->khe/dot_general | solution.py:114
  363.6 3.2 fusion.143
  370.2 1.7 constant_dynamic-slice_fusion.11
  373.1 2.8 fusion.141
  375.8 5.4 %fusion.142 = f32[16,64,128]{2,1,0:T(8,128)S(1)} fusion(bf16[512,16,64]{0,2,1:T(8,128)(2,1)S(1)} %bitcast.339, f32[16,512,128]{2,1,0:T(8,128)} %fusion.141, bf16[512,16,64]{0,2,1:T(8,128)(2,1)S(1)} %bitcast.340, bf16[128,16,64]{0,2,1:T(8,128)(2,1)} %get-tuple-element.576, f32[512,16]{0,1:T(8,128)S(1)} %bitcast.359, f32[512,16]{0,1:T(8,128)S(1)} %bitcast.357, ...), kind=kOutput, calls=%fused_computation.13.clone.1 | convolution fusion | flops 274857984 | bytes 7208960 | tf_op jit(solution)/shard_map/while/body/eval_jaxpr/qhk,qhe->khe/dot_general | solution.py:114
  381.2 3.2 fusion.143
  387.8 1.7 constant_dynamic-slice_fusion.11
  390.6 2.8 fusion.141
  393.4 5.4 %fusion.142 = f32[16,64,128]{2,1,0:T(8,128)S(1)} fusion(bf16[512,16,64]{0,2,1:T(8,128)(2,1)S(1)} %bitcast.339, f32[16,512,128]{2,1,0:T(8,128)} %fusion.141, bf16[512,16,64]{0,2,1:T(8,128)(2,1)S(1)} %bitcast.340, bf16[128,16,64]{0,2,1:T(8,128)(2,1)} %get-tuple-element.576, f32[512,16]{0,1:T(8,128)S(1)} %bitcast.359, f32[512,16]{0,1:T(8,128)S(1)} %bitcast.357, ...), kind=kOutput, calls=%fused_computation.13.clone.1 | convolution fusion | flops 274857984 | bytes 7208960 | tf_op jit(solution)/shard_map/while/body/eval_jaxpr/qhk,qhe->khe/dot_general | solution.py:114
  398.7 3.2 fusion.143
  404.6 1.8 fusion.37
  (332 shorter events, 119.3 us)
Async XLA Ops:
  6.5 111.7 %all-gather.12.cloned.1.call-start = ((), (), s32[]{:S(2)}) async-start(), calls=%async_computation.2 | async-start | bytes 8650752 | tf_op jit(solution)/shard_map/all_gather | solution.py:164
  7.3 243.6 %all-gather.8.cloned.1.call-start = ((), (), s32[]{:S(2)}) async-start(), calls=%async_computation | async-start | bytes 8650752 | tf_op jit(solution)/shard_map/all_gather | solution.py:211
  8.4 11.5 %collective-permute-start = (bf16[128,1024]{0,1:T(8,128)(2,1)S(1)}, bf16[128,1024]{0,1:T(8,128)(2,1)S(1)}, u32[]{:S(2)}, u32[]{:S(2)}) collective-permute-start(bf16[128,1024]{0,1:T(8,128)(2,1)S(1)} %bitcast.363), channel_id=1, source_target_pairs={{32,0},{64,32},{96,64},{128,96},{160,128},{192,160},{224,192},{33,... | collective-permute-start | bytes 786440 | tf_op jit(solution)/shard_map/ppermute | solution.py:19
  20.6 91.2 %copy-start.2 = (bf16[128,1024]{0,1:T(8,128)(2,1)S(1)}, bf16[128,1024]{0,1:T(8,128)(2,1)}, u32[]{:S(2)}) copy-start(bf16[128,1024]{0,1:T(8,128)(2,1)} %broadcast_select_fusion) | copy-start | bytes 786436
  20.7 242.2 %all-gather.10.cloned.1.call-start = ((), (), s32[]{:S(2)}) async-start(), calls=%async_computation.1 | async-start | bytes 8650752 | tf_op jit(solution)/shard_map/all_gather | solution.py:210
  29.7 82.0 %collective-permute-start.1 = (bf16[64,1024]{0,1:T(8,128)(2,1)S(1)}, bf16[64,1024]{0,1:T(8,128)(2,1)S(1)}, u32[]{:S(2)}, u32[]{:S(2)}) collective-permute-start(bf16[64,1024]{0,1:T(8,128)(2,1)S(1)} %get-tuple-element.327), channel_id=1, source_target_pairs={{0,1},{1,2},{2,3},{3,4},{4,5},{5,6},{6,7},{7,8},{8,9},{9,10},{10,1... | collective-permute-start | bytes 393224 | tf_op jit(solution)/shard_map/ppermute | solution.py:27
  34.7 77.1 %collective-permute-start.2 = (bf16[64,1024]{0,1:T(8,128)(2,1)S(1)}, bf16[64,1024]{0,1:T(8,128)(2,1)S(1)}, u32[]{:S(2)}, u32[]{:S(2)}) collective-permute-start(bf16[64,1024]{0,1:T(8,128)(2,1)S(1)} %get-tuple-element.328), channel_id=1, source_target_pairs={{1,0},{2,1},{3,2},{4,3},{5,4},{6,5},{7,6},{8,7},{9,8},{10,9},{11,1... | collective-permute-start | bytes 393224 | tf_op jit(solution)/shard_map/ppermute | solution.py:30
  113.8 1.5 copy-start.3
  115.0 3.3 copy-start.4
  115.0 3.3 copy-start.5
  115.0 3.3 copy-start.6
  270.4 8.7 %copy-start = (f32[128,1024]{0,1:T(8,128)S(1)}, f32[128,1024]{0,1:T(8,128)}, u32[]{:S(2)}) copy-start(f32[128,1024]{0,1:T(8,128)} %get-tuple-element.555) | copy-start | bytes 1572868 | tf_op jit(solution)/shard_map/while
  279.6 0.8 copy-start.1
  288.0 8.7 %copy-start = (f32[128,1024]{0,1:T(8,128)S(1)}, f32[128,1024]{0,1:T(8,128)}, u32[]{:S(2)}) copy-start(f32[128,1024]{0,1:T(8,128)} %get-tuple-element.555) | copy-start | bytes 1572868 | tf_op jit(solution)/shard_map/while
  297.2 0.8 copy-start.1
  305.6 8.7 %copy-start = (f32[128,1024]{0,1:T(8,128)S(1)}, f32[128,1024]{0,1:T(8,128)}, u32[]{:S(2)}) copy-start(f32[128,1024]{0,1:T(8,128)} %get-tuple-element.555) | copy-start | bytes 1572868 | tf_op jit(solution)/shard_map/while
  314.8 0.8 copy-start.1
  323.1 8.7 %copy-start = (f32[128,1024]{0,1:T(8,128)S(1)}, f32[128,1024]{0,1:T(8,128)}, u32[]{:S(2)}) copy-start(f32[128,1024]{0,1:T(8,128)} %get-tuple-element.555) | copy-start | bytes 1572868 | tf_op jit(solution)/shard_map/while
  332.3 0.8 copy-start.1
  340.7 8.7 %copy-start = (f32[128,1024]{0,1:T(8,128)S(1)}, f32[128,1024]{0,1:T(8,128)}, u32[]{:S(2)}) copy-start(f32[128,1024]{0,1:T(8,128)} %get-tuple-element.555) | copy-start | bytes 1572868 | tf_op jit(solution)/shard_map/while
  349.9 0.8 copy-start.1
  358.3 8.7 %copy-start = (f32[128,1024]{0,1:T(8,128)S(1)}, f32[128,1024]{0,1:T(8,128)}, u32[]{:S(2)}) copy-start(f32[128,1024]{0,1:T(8,128)} %get-tuple-element.555) | copy-start | bytes 1572868 | tf_op jit(solution)/shard_map/while
  367.5 0.8 copy-start.1
  375.8 8.7 %copy-start = (f32[128,1024]{0,1:T(8,128)S(1)}, f32[128,1024]{0,1:T(8,128)}, u32[]{:S(2)}) copy-start(f32[128,1024]{0,1:T(8,128)} %get-tuple-element.555) | copy-start | bytes 1572868 | tf_op jit(solution)/shard_map/while
  385.0 0.8 copy-start.1
  393.4 8.7 %copy-start = (f32[128,1024]{0,1:T(8,128)S(1)}, f32[128,1024]{0,1:T(8,128)}, u32[]{:S(2)}) copy-start(f32[128,1024]{0,1:T(8,128)} %get-tuple-element.555) | copy-start | bytes 1572868 | tf_op jit(solution)/shard_map/while
  402.6 0.8 copy-start.1
Sparse Core Ops, SparseCore 0:
  9.2 76.3 all-gather.11
  87.3 89.5 all-gather.7
  178.8 70.4 all-gather.9
where the time goes:
time: 415 us; the launch traced here: 413 us
  blocking collectives  135 us (33%)
  matrix products  114 us (27%)
  local copies, waits for them, and re-layouts  94.4 us (23%)
  other arithmetic  34.7 us (8%)
  between operations  13.6 us (3%)
  starting transfers between devices  9.84 us (2%)
  waiting for transfers between devices  8.88 us (2%)
    dot_general x8, matrix products, key_terms(): jnp.einsum('qhk,qhe->khe', score_grad, query_heads, preferred_element_typ...  42.9 us
    all_gather x1, blocking collectives, on_device(): lax.all_gather(time_wire, 'ctx', axis=0, tiled=True)  39.2 us
    dynamic_slice x40, local copies, waits for them, and re-layouts, on_device(): lax.scan(sweep_keys, running, (segment_x.reshape(length // block_size, bl...  37.2 us
    all_gather x1, blocking collectives, on_device(): lax.all_gather(delta_rows, 'ctx', axis=0, tiled=True)  33.4 us
    all_gather x1, blocking collectives, on_device(): lax.all_gather(log_total, 'ctx', axis=0, tiled=True)  32.4 us
    dot_general x16, matrix products, masked_scores(): jnp.einsum('qhe,khe->qhk', query_heads, key_heads, preferred_element_type...  31.2 us
    all_gather x1, blocking collectives, on_device(): lax.all_gather(own_times, 'ctx', axis=0, tiled=True)  30.5 us
    dot_general x8, matrix products, key_terms(): jnp.einsum('qhk,qhe->khe', probability.astype(jnp.bfloat16), grad_heads,...  25.7 us
  transfers between devices with their start and end apart: 6, of which 1 were waited for; matrix products, arithmetic and copies ran while one was open for 24% of the time, Pallas kernels for 0%

commit v1 on v0

--- a/solution.py
+++ b/solution.py
@@ -208,7 +208,9 @@
     accumulated = jnp.zeros((row_count, feature_count), jnp.float32)
     shard_part = (
         lax.all_gather(own_queries, "ctx", axis=0, tiled=True),
-        lax.all_gather(incoming, "ctx", axis=0, tiled=True),
+        jnp.concatenate(
+            lax.all_to_all(jnp.stack([incoming] * lax.axis_size("ctx")), "ctx", 0, 0), axis=0
+        ),
     )
     length = shard_part[0].shape[0]
     block_size = math.gcd(length, 512)

time: 415 us -> 560 us (1.35)
  blocking collectives: 135 us -> 221 us
  matrix products: 114 us -> 162 us
  other arithmetic: 34.7 us -> 57.4 us
  local copies, waits for them, and re-layouts: 94.4 us -> 82.4 us
  waiting for transfers between devices: 8.88 us -> 0.74 us
    all_gather x1, blocking collectives: 32.4 us -> 122 us  [on_device(): lax.all_gather(log_total, 'ctx', axis=0, tiled=True)]
    dot_general x16, matrix products: 31.2 us -> 55.1 us  [masked_scores(): jnp.einsum('qhe,khe->qhk', query_heads, key_heads, preferred_element_type...]
    reduce_sum x8, other arithmetic: 7.07 us -> 24.4 us  [running_stats(): jnp.sum(exponent, axis=2)]
    dot_general x8, matrix products: 12.8 us -> 29.8 us  [running_stats(): jnp.einsum('qhe,khe->qhk', grad_heads, value_heads, preferred_element_typ...]
    all_gather x1 -> x0, local copies, waits for them, and re-layouts: 12 us -> none  [on_device(): lax.all_gather(incoming, 'ctx', axis=0, tiled=True)]
    add x8, other arithmetic: 4.1 us -> 12.6 us  [sweep_queries(): accumulated + key_terms(split_heads(segment_q), split_heads(segment_g), s...]
    ppermute x1, waiting for transfers between devices: 7.46 us -> 0.01 us  [shifted(): lax.ppermute(value, axis, [(source, source + steps) for source in range(l...]
    dot_general x8, matrix products: 42.9 us -> 49.8 us  [key_terms(): jnp.einsum('qhk,qhe->khe', score_grad, query_heads, preferred_element_typ...]
  transfers between devices with their start and end apart: 6 -> 6, of which waited for: 1 -> 0; matrix products, arithmetic and copies ran while one was open for 24% -> 26% of each run, Pallas kernels for 0% -> 0%
where the time goes in v1:
time: 560 us; the launch traced here: 554 us
  blocking collectives  221 us (39%)
  matrix products  162 us (29%)
  local copies, waits for them, and re-layouts  82.4 us (15%)
  other arithmetic  57.4 us (10%)
  starting transfers between devices  15.1 us (3%)
  between operations  13.8 us (2%)
    all_gather x1, blocking collectives, on_device(): lax.all_gather(log_total, 'ctx', axis=0, tiled=True)  122 us
    dot_general x16, matrix products, masked_scores(): jnp.einsum('qhe,khe->qhk', query_heads, key_heads, preferred_element_type...  55.1 us
    dot_general x8, matrix products, key_terms(): jnp.einsum('qhk,qhe->khe', score_grad, query_heads, preferred_element_typ...  49.8 us
    dynamic_slice x40, local copies, waits for them, and re-layouts, on_device(): lax.scan(sweep_keys, running, (segment_x.reshape(length // block_size, bl...  37.1 us
    all_gather x1, blocking collectives, on_device(): lax.all_gather(time_wire, 'ctx', axis=0, tiled=True)  36.2 us
    all_gather x1, blocking collectives, on_device(): lax.all_gather(delta_rows, 'ctx', axis=0, tiled=True)  31.6 us
    all_gather x1, blocking collectives, on_device(): lax.all_gather(own_times, 'ctx', axis=0, tiled=True)  30.4 us
    dot_general x8, matrix products, running_stats(): jnp.einsum('qhe,khe->qhk', grad_heads, value_heads, preferred_element_typ...  29.8 us
  transfers between devices with their start and end apart: 6, of which 0 were waited for; matrix products, arithmetic and copies ran while one was open for 26% of the time, Pallas kernels for 0%

profile of v1, /device:TPU:29, one launch (start us, length us, event | category | flops | bytes accessed | tf_op | source)
XLA Modules:
  0.0 554.2 jit_solution(10740507614252324934)
XLA Ops:
  19.6 4.4 collective-permute-start.1
  26.0 36.2 %all-gather.2 = bf16[1,4096]{1,0:T(2,128)(2,1)S(1)} all-gather(bf16[1,128]{1,0:T(2,128)(2,1)S(1)} %get-tuple-element.308), channel_id=4, replica_groups=mesh['pipe'=8,'ctx'=32] {'ctx'}, dimensions={1}, use_global_device_ids=true | all-gather | bytes 8448 | tf_op jit(solution)/shard_map/all_gather | solution.py:165
  63.5 30.4 %all-gather.1 = f32[1,4096]{1,0:T(1,128)S(1)} all-gather(f32[1,128]{1,0:T(1,128)S(1)} %get-tuple-element.310), channel_id=3, replica_groups=mesh['pipe'=8,'ctx'=32] {'ctx'}, dimensions={1}, use_global_device_ids=true | all-gather | bytes 16896 | tf_op jit(solution)/shard_map/all_gather | solution.py:185
  96.1 4.3 stack.147
  100.4 5.8 %all-to-all-start = ((bf16[32,128,1024]{2,1,0:T(8,128)(2,1)}), bf16[32,128,1024]{2,1,0:T(8,128)(2,1)}, u32[]{:S(2)}, u32[]{:S(2)}) async-start(bf16[32,128,1024]{2,1,0:T(8,128)(2,1)} %stack.147), calls=%async_computation | async-start | bytes 16777216 | tf_op jit(solution)/shard_map/all_to_all | solution.py:212
  111.5 121.4 %while.26 = (s32[]{:T(128)}, f32[128,16]{0,1:T(8,128)S(1)}, f32[128,16]{0,1:T(8,128)S(1)}, f32[128,16]{0,1:T(8,128)S(1)}, bf16[8,512]{1,0:T(8,128)(2,1)S(1)}, /*...) while((s32[]{:T(128)}, f32[128,16]{0,1:T(8,128)S(1)}, ...), condition=%wide.region_4.5_spmd.clone, body=%wide.region_0.4_spmd.clone.sunk | while | flops 284768768 | bytes 25097924 | solution.py:171
  114.6 4.2 fusion.131
  118.8 3.1 fusion.135
  122.9 3.7 fusion.134
  129.8 4.2 fusion.131
  134.0 3.0 fusion.135
  138.1 3.7 fusion.134
  145.0 4.2 fusion.131
  149.1 3.0 fusion.135
  153.2 3.7 fusion.134
  160.1 4.2 fusion.131
  164.3 3.0 fusion.135
  168.4 3.7 fusion.134
  175.3 4.2 fusion.131
  179.5 3.1 fusion.135
  183.6 3.7 fusion.134
  190.5 4.2 fusion.131
  194.7 3.0 fusion.135
  198.8 3.7 fusion.134
  205.7 4.2 fusion.131
  214.0 3.7 fusion.134
  220.8 4.2 fusion.131
  225.0 3.1 fusion.135
  229.1 3.7 fusion.134
  232.9 122.4 %all_gather.22 = f32[4096,16]{0,1:T(8,128)S(1)} all-gather(f32[128,16]{0,1:T(8,128)S(1)} %get-tuple-element.307), channel_id=1, replica_groups=mesh['pipe'=8,'ctx'=32] {'ctx'}, dimensions={0}, use_global_device_ids=true | all-gather | bytes 270336 | tf_op jit(solution)/shard_map/all_gather | solution.py:183
  356.2 31.6 %all_gather.23 = f32[4096,16]{0,1:T(8,128)S(1)} all-gather(f32[128,16]{0,1:T(8,128)S(1)} %get-tuple-element.306), channel_id=1, replica_groups=mesh['pipe'=8,'ctx'=32] {'ctx'}, dimensions={0}, use_global_device_ids=true | all-gather | bytes 270336 | tf_op jit(solution)/shard_map/all_gather | solution.py:184
  388.7 155.6 %while.27 = (s32[]{:T(128)}, f32[128,1024]{0,1:T(8,128)}, bf16[8,512,1024]{2,1,0:T(8,128)(2,1)}, f32[128]{0:T(128)S(1)}, f32[8,512]{1,0:T(8,128)}, /*index=5*/bf...) while((s32[]{:T(128)}, f32[128,1024]{0,1:T(8,128)}, ...), condition=%wide.region_6.7_spmd.clone, body=%wide.region_5.6_spmd.clone.sunk | while | flops 548339712 | bytes 35699408 | solution.py:225
  396.2 3.2 fusion.146
  399.5 6.2 %fusion.145 = f32[16,64,128]{2,1,0:T(8,128)} fusion(bf16[512,16,64]{0,2,1:T(8,128)(2,1)S(1)} %bitcast.339, f32[16,512,128]{2,1,0:T(8,128)} %fusion.144, bf16[512,16,64]{0,2,1:T(8,128)(2,1)S(1)} %bitcast.341, f32[512,16]{0,1:T(8,128)S(1)} %bitcast.354, f32[512,16]{0,1:T(8,128)S(1)} %bitcast.353, pred[512,128]{1,0:T(8,128)(4,1)S(1)} %broadcast_compare_fusion.5, ...), kind=kOutput, calls=%fused_computation.13.clone.1 | convolution fusion | flops 274857984 | bytes 7208960 | tf_op jit(solution)/shard_map/while/body/eval_jaxpr/qhk,qhe->khe/dot_general | solution.py:114
  415.6 3.2 fusion.146
  419.0 6.2 %fusion.145 = f32[16,64,128]{2,1,0:T(8,128)} fusion(bf16[512,16,64]{0,2,1:T(8,128)(2,1)S(1)} %bitcast.339, f32[16,512,128]{2,1,0:T(8,128)} %fusion.144, bf16[512,16,64]{0,2,1:T(8,128)(2,1)S(1)} %bitcast.341, f32[512,16]{0,1:T(8,128)S(1)} %bitcast.354, f32[512,16]{0,1:T(8,128)S(1)} %bitcast.353, pred[512,128]{1,0:T(8,128)(4,1)S(1)} %broadcast_compare_fusion.5, ...), kind=kOutput, calls=%fused_computation.13.clone.1 | convolution fusion | flops 274857984 | bytes 7208960 | tf_op jit(solution)/shard_map/while/body/eval_jaxpr/qhk,qhe->khe/dot_general | solution.py:114
  435.1 3.2 fusion.146
  438.4 6.2 %fusion.145 = f32[16,64,128]{2,1,0:T(8,128)} fusion(bf16[512,16,64]{0,2,1:T(8,128)(2,1)S(1)} %bitcast.339, f32[16,512,128]{2,1,0:T(8,128)} %fusion.144, bf16[512,16,64]{0,2,1:T(8,128)(2,1)S(1)} %bitcast.341, f32[512,16]{0,1:T(8,128)S(1)} %bitcast.354, f32[512,16]{0,1:T(8,128)S(1)} %bitcast.353, pred[512,128]{1,0:T(8,128)(4,1)S(1)} %broadcast_compare_fusion.5, ...), kind=kOutput, calls=%fused_computation.13.clone.1 | convolution fusion | flops 274857984 | bytes 7208960 | tf_op jit(solution)/shard_map/while/body/eval_jaxpr/qhk,qhe->khe/dot_general | solution.py:114
  454.5 3.2 fusion.146
  457.9 6.2 %fusion.145 = f32[16,64,128]{2,1,0:T(8,128)} fusion(bf16[512,16,64]{0,2,1:T(8,128)(2,1)S(1)} %bitcast.339, f32[16,512,128]{2,1,0:T(8,128)} %fusion.144, bf16[512,16,64]{0,2,1:T(8,128)(2,1)S(1)} %bitcast.341, f32[512,16]{0,1:T(8,128)S(1)} %bitcast.354, f32[512,16]{0,1:T(8,128)S(1)} %bitcast.353, pred[512,128]{1,0:T(8,128)(4,1)S(1)} %broadcast_compare_fusion.5, ...), kind=kOutput, calls=%fused_computation.13.clone.1 | convolution fusion | flops 274857984 | bytes 7208960 | tf_op jit(solution)/shard_map/while/body/eval_jaxpr/qhk,qhe->khe/dot_general | solution.py:114
  474.0 3.2 fusion.146
  477.3 6.2 %fusion.145 = f32[16,64,128]{2,1,0:T(8,128)} fusion(bf16[512,16,64]{0,2,1:T(8,128)(2,1)S(1)} %bitcast.339, f32[16,512,128]{2,1,0:T(8,128)} %fusion.144, bf16[512,16,64]{0,2,1:T(8,128)(2,1)S(1)} %bitcast.341, f32[512,16]{0,1:T(8,128)S(1)} %bitcast.354, f32[512,16]{0,1:T(8,128)S(1)} %bitcast.353, pred[512,128]{1,0:T(8,128)(4,1)S(1)} %broadcast_compare_fusion.5, ...), kind=kOutput, calls=%fused_computation.13.clone.1 | convolution fusion | flops 274857984 | bytes 7208960 | tf_op jit(solution)/shard_map/while/body/eval_jaxpr/qhk,qhe->khe/dot_general | solution.py:114
  493.4 3.2 fusion.146
  496.8 6.2 %fusion.145 = f32[16,64,128]{2,1,0:T(8,128)} fusion(bf16[512,16,64]{0,2,1:T(8,128)(2,1)S(1)} %bitcast.339, f32[16,512,128]{2,1,0:T(8,128)} %fusion.144, bf16[512,16,64]{0,2,1:T(8,128)(2,1)S(1)} %bitcast.341, f32[512,16]{0,1:T(8,128)S(1)} %bitcast.354, f32[512,16]{0,1:T(8,128)S(1)} %bitcast.353, pred[512,128]{1,0:T(8,128)(4,1)S(1)} %broadcast_compare_fusion.5, ...), kind=kOutput, calls=%fused_computation.13.clone.1 | convolution fusion | flops 274857984 | bytes 7208960 | tf_op jit(solution)/shard_map/while/body/eval_jaxpr/qhk,qhe->khe/dot_general | solution.py:114
  512.9 3.2 fusion.146
  516.2 6.2 %fusion.145 = f32[16,64,128]{2,1,0:T(8,128)} fusion(bf16[512,16,64]{0,2,1:T(8,128)(2,1)S(1)} %bitcast.339, f32[16,512,128]{2,1,0:T(8,128)} %fusion.144, bf16[512,16,64]{0,2,1:T(8,128)(2,1)S(1)} %bitcast.341, f32[512,16]{0,1:T(8,128)S(1)} %bitcast.354, f32[512,16]{0,1:T(8,128)S(1)} %bitcast.353, pred[512,128]{1,0:T(8,128)(4,1)S(1)} %broadcast_compare_fusion.5, ...), kind=kOutput, calls=%fused_computation.13.clone.1 | convolution fusion | flops 274857984 | bytes 7208960 | tf_op jit(solution)/shard_map/while/body/eval_jaxpr/qhk,qhe->khe/dot_general | solution.py:114
  532.3 3.2 fusion.146
  535.7 6.2 %fusion.145 = f32[16,64,128]{2,1,0:T(8,128)} fusion(bf16[512,16,64]{0,2,1:T(8,128)(2,1)S(1)} %bitcast.339, f32[16,512,128]{2,1,0:T(8,128)} %fusion.144, bf16[512,16,64]{0,2,1:T(8,128)(2,1)S(1)} %bitcast.341, f32[512,16]{0,1:T(8,128)S(1)} %bitcast.354, f32[512,16]{0,1:T(8,128)S(1)} %bitcast.353, pred[512,128]{1,0:T(8,128)(4,1)S(1)} %broadcast_compare_fusion.5, ...), kind=kOutput, calls=%fused_computation.13.clone.1 | convolution fusion | flops 274857984 | bytes 7208960 | tf_op jit(solution)/shard_map/while/body/eval_jaxpr/qhk,qhe->khe/dot_general | solution.py:114
  (337 shorter events, 143.6 us)
Async XLA Ops:
  6.5 105.0 %all-gather.9.cloned.1.call-start = ((), (), s32[]{:S(2)}) async-start(), calls=%async_computation.2 | async-start | bytes 8650752 | tf_op jit(solution)/shard_map/all_gather | solution.py:164
  7.3 381.4 %all-gather.7.cloned.1.call-start = ((), (), s32[]{:S(2)}) async-start(), calls=%async_computation.1 | async-start | bytes 8650752 | tf_op jit(solution)/shard_map/all_gather | solution.py:210
  7.3 12.2 %collective-permute-start = (bf16[128,1024]{1,0:T(8,128)(2,1)}, bf16[128,1024]{1,0:T(8,128)(2,1)S(1)}, u32[]{:S(2)}, u32[]{:S(2)}) collective-permute-start(bf16[128,1024]{1,0:T(8,128)(2,1)} %bitcast.364), channel_id=1, source_target_pairs={{32,0},{64,32},{96,64},{128,96},{160,128},{192,160},{224,192},{33,... | collective-permute-start | bytes 786440 | tf_op jit(solution)/shard_map/ppermute | solution.py:19
  19.6 86.6 %collective-permute-start.1 = (bf16[64,1024]{1,0:T(8,128)(2,1)S(1)}, bf16[64,1024]{1,0:T(8,128)(2,1)S(1)}, u32[]{:S(2)}, u32[]{:S(2)}) collective-permute-start(bf16[64,1024]{1,0:T(8,128)(2,1)S(1)} %get-tuple-element.304), channel_id=1, source_target_pairs={{0,1},{1,2},{2,3},{3,4},{4,5},{5,6},{6,7},{7,8},{8,9},{9,10},{10,1... | collective-permute-start | bytes 393224 | tf_op jit(solution)/shard_map/ppermute | solution.py:27
  24.0 82.2 %collective-permute-start.2 = (bf16[64,1024]{1,0:T(8,128)(2,1)S(1)}, bf16[64,1024]{1,0:T(8,128)(2,1)S(1)}, u32[]{:S(2)}, u32[]{:S(2)}) collective-permute-start(bf16[64,1024]{1,0:T(8,128)(2,1)S(1)} %get-tuple-element.305), channel_id=1, source_target_pairs={{1,0},{2,1},{3,2},{4,3},{5,4},{6,5},{7,6},{8,7},{9,8},{10,9},{11,1... | collective-permute-start | bytes 393224 | tf_op jit(solution)/shard_map/ppermute | solution.py:30
  100.4 288.3 %all-to-all-start = ((bf16[32,128,1024]{2,1,0:T(8,128)(2,1)}), bf16[32,128,1024]{2,1,0:T(8,128)(2,1)}, u32[]{:S(2)}, u32[]{:S(2)}) async-start(bf16[32,128,1024]{2,1,0:T(8,128)(2,1)} %stack.147), calls=%async_computation | async-start | bytes 16777216 | tf_op jit(solution)/shard_map/all_to_all | solution.py:212
  108.3 3.2 copy-start.2
  108.3 3.2 copy-start.3
  114.6 8.3 %copy-start.4 = (bf16[128,16,64]{0,2,1:T(8,128)(2,1)S(1)}, bf16[128,16,64]{0,2,1:T(8,128)(2,1)}, u32[]{:S(2)}) copy-start(bf16[128,16,64]{0,2,1:T(8,128)(2,1)} %get-tuple-element.513) | copy-start | bytes 786436 | tf_op jit(solution)/shard_map/while
  129.8 8.3 %copy-start.4 = (bf16[128,16,64]{0,2,1:T(8,128)(2,1)S(1)}, bf16[128,16,64]{0,2,1:T(8,128)(2,1)}, u32[]{:S(2)}) copy-start(bf16[128,16,64]{0,2,1:T(8,128)(2,1)} %get-tuple-element.513) | copy-start | bytes 786436 | tf_op jit(solution)/shard_map/while
  145.0 8.3 %copy-start.4 = (bf16[128,16,64]{0,2,1:T(8,128)(2,1)S(1)}, bf16[128,16,64]{0,2,1:T(8,128)(2,1)}, u32[]{:S(2)}) copy-start(bf16[128,16,64]{0,2,1:T(8,128)(2,1)} %get-tuple-element.513) | copy-start | bytes 786436 | tf_op jit(solution)/shard_map/while
  160.1 8.3 %copy-start.4 = (bf16[128,16,64]{0,2,1:T(8,128)(2,1)S(1)}, bf16[128,16,64]{0,2,1:T(8,128)(2,1)}, u32[]{:S(2)}) copy-start(bf16[128,16,64]{0,2,1:T(8,128)(2,1)} %get-tuple-element.513) | copy-start | bytes 786436 | tf_op jit(solution)/shard_map/while
  175.3 8.3 %copy-start.4 = (bf16[128,16,64]{0,2,1:T(8,128)(2,1)S(1)}, bf16[128,16,64]{0,2,1:T(8,128)(2,1)}, u32[]{:S(2)}) copy-start(bf16[128,16,64]{0,2,1:T(8,128)(2,1)} %get-tuple-element.513) | copy-start | bytes 786436 | tf_op jit(solution)/shard_map/while
  190.5 8.3 %copy-start.4 = (bf16[128,16,64]{0,2,1:T(8,128)(2,1)S(1)}, bf16[128,16,64]{0,2,1:T(8,128)(2,1)}, u32[]{:S(2)}) copy-start(bf16[128,16,64]{0,2,1:T(8,128)(2,1)} %get-tuple-element.513) | copy-start | bytes 786436 | tf_op jit(solution)/shard_map/while
  205.7 8.3 %copy-start.4 = (bf16[128,16,64]{0,2,1:T(8,128)(2,1)S(1)}, bf16[128,16,64]{0,2,1:T(8,128)(2,1)}, u32[]{:S(2)}) copy-start(bf16[128,16,64]{0,2,1:T(8,128)(2,1)} %get-tuple-element.513) | copy-start | bytes 786436 | tf_op jit(solution)/shard_map/while
  220.8 8.3 %copy-start.4 = (bf16[128,16,64]{0,2,1:T(8,128)(2,1)S(1)}, bf16[128,16,64]{0,2,1:T(8,128)(2,1)}, u32[]{:S(2)}) copy-start(bf16[128,16,64]{0,2,1:T(8,128)(2,1)} %get-tuple-element.513) | copy-start | bytes 786436 | tf_op jit(solution)/shard_map/while
  399.4 6.4 %copy-start = (f32[128,1024]{0,1:T(8,128)S(1)}, f32[128,1024]{0,1:T(8,128)}, u32[]{:S(2)}) copy-start(f32[128,1024]{0,1:T(8,128)} %get-tuple-element.532) | copy-start | bytes 1572868 | tf_op jit(solution)/shard_map/while
  407.3 0.8 copy-start.1
  418.8 6.4 %copy-start = (f32[128,1024]{0,1:T(8,128)S(1)}, f32[128,1024]{0,1:T(8,128)}, u32[]{:S(2)}) copy-start(f32[128,1024]{0,1:T(8,128)} %get-tuple-element.532) | copy-start | bytes 1572868 | tf_op jit(solution)/shard_map/while
  426.8 0.8 copy-start.1
  438.3 6.4 %copy-start = (f32[128,1024]{0,1:T(8,128)S(1)}, f32[128,1024]{0,1:T(8,128)}, u32[]{:S(2)}) copy-start(f32[128,1024]{0,1:T(8,128)} %get-tuple-element.532) | copy-start | bytes 1572868 | tf_op jit(solution)/shard_map/while
  446.2 0.8 copy-start.1
  457.7 6.4 %copy-start = (f32[128,1024]{0,1:T(8,128)S(1)}, f32[128,1024]{0,1:T(8,128)}, u32[]{:S(2)}) copy-start(f32[128,1024]{0,1:T(8,128)} %get-tuple-element.532) | copy-start | bytes 1572868 | tf_op jit(solution)/shard_map/while
  465.7 0.8 copy-start.1
  477.2 6.4 %copy-start = (f32[128,1024]{0,1:T(8,128)S(1)}, f32[128,1024]{0,1:T(8,128)}, u32[]{:S(2)}) copy-start(f32[128,1024]{0,1:T(8,128)} %get-tuple-element.532) | copy-start | bytes 1572868 | tf_op jit(solution)/shard_map/while
  485.1 0.8 copy-start.1
  496.6 6.4 %copy-start = (f32[128,1024]{0,1:T(8,128)S(1)}, f32[128,1024]{0,1:T(8,128)}, u32[]{:S(2)}) copy-start(f32[128,1024]{0,1:T(8,128)} %get-tuple-element.532) | copy-start | bytes 1572868 | tf_op jit(solution)/shard_map/while
  504.6 0.8 copy-start.1
  516.1 6.4 %copy-start = (f32[128,1024]{0,1:T(8,128)S(1)}, f32[128,1024]{0,1:T(8,128)}, u32[]{:S(2)}) copy-start(f32[128,1024]{0,1:T(8,128)} %get-tuple-element.532) | copy-start | bytes 1572868 | tf_op jit(solution)/shard_map/while
  524.0 0.8 copy-start.1
  535.6 6.4 %copy-start = (f32[128,1024]{0,1:T(8,128)S(1)}, f32[128,1024]{0,1:T(8,128)}, u32[]{:S(2)}) copy-start(f32[128,1024]{0,1:T(8,128)} %get-tuple-element.532) | copy-start | bytes 1572868 | tf_op jit(solution)/shard_map/while
  543.5 0.8 copy-start.1
Sparse Core Ops, SparseCore 0:
  9.2 75.7 all-gather.8
  86.8 178.4 all-gather.6
